TPU v7x, 32 devices: a whole 2x2x4 slice. The times are simulated.
32 devices in a mesh: cuts: 2 (over y), inter: 16 (over z, x, core).
Axes of the slice: x: 2, y: 2, z: 4, core: 2. Of those that a mesh axis runs over, the one named last changes fastest.
Arguments:
- stem_tensor: bfloat16 [2, 1024, 512, 1, 256], P(None, ('cuts', 'inter')), parts along dimension 1, may hold values from -6 to 6
- branch_one: bfloat16 [2, 512, 512], replicated, may hold values from -0.1875 to 0.1875
- branch_two: bfloat16 [2, 256, 256], replicated, may hold values from -0.25 to 0.25
- mode_order: int32 [256], replicated, may hold values from 0 to 255, each once
- branch_three: bfloat16 [2, 512, 512], replicated, may hold values from -0.1875 to 0.1875
- closing: bfloat16 [2, 512, 512], replicated, may hold values from -4 to 4
Outputs:
- amplitudes: float32 [1024, 512, 2, 1, 256], P(('cuts', 'inter')), parts along dimension 0
There are 2 independent parts, one for each index of `cuts`. A program takes and returns all parts, laid end to end along the dimension named above; an argument that names none is the same for every part. Nothing has to cross between parts.
All inputs are finite; a program needn't handle non-finite values.
Results may differ from a plain program's by a relative error of at most 0.0041.
Values may be sent and summed in bfloat16 or wider, within the bound.
A program may use at most 192 MiB of HBM per device.

v0:
```python
import jax
import jax.numpy as jnp
from jax import lax
from jax.sharding import PartitionSpec as P


def complex_mix(input_real, input_imag, weight_real, weight_imag, pattern):

    def product(first_op, second_op):
        return jnp.einsum(pattern, first_op, second_op, preferred_element_type=jnp.float32)

    return (
        product(input_real, weight_real) - product(input_imag, weight_imag),
        product(input_real, weight_imag) + product(input_imag, weight_real),
    )


def on_device(stem_tensor, branch_one, branch_two, mode_order, branch_three, closing):
    group_size = lax.axis_size("inter")
    my_index = lax.axis_index("inter")
    local_b = branch_three.shape[1] // group_size
    permuted = jnp.zeros_like(branch_two).at[:, mode_order, :].set(branch_two)
    close_cols = lax.dynamic_slice_in_dim(closing, my_index * local_b, local_b, 2).astype(
        jnp.float32
    )
    close_real = close_cols[0][:, :, None, None]
    close_imag = close_cols[1][:, :, None, None]
    received = lax.all_to_all(stem_tensor, "inter", split_axis=2, concat_axis=1, tiled=True)
    real_part, imag_part = complex_mix(
        received[0], received[1], branch_one[0], branch_one[1], "abkr,ac->cbkr"
    )
    phased = jnp.stack(
        [
            close_real * real_part - close_imag * imag_part,
            close_real * imag_part + close_imag * real_part,
        ]
    ).astype(jnp.bfloat16)
    real_two, imag_two = complex_mix(
        phased[0], phased[1], permuted[0], permuted[1], "abkr,rq->abkq"
    )
    second = jnp.stack([real_two, imag_two]).astype(jnp.bfloat16)
    returned = lax.all_to_all(second, "inter", split_axis=1, concat_axis=2, tiled=True)
    out_real, out_imag = complex_mix(
        returned[0], returned[1], branch_three[0], branch_three[1], "abkr,bc->ackr"
    )
    return jnp.stack([out_real, out_imag], axis=2)


def solution(mesh):
    in_specs = (P(None, ("cuts", "inter"), None, None, None), P(), P(), P(), P(), P())
    out_specs = P(("cuts", "inter"), None, None, None, None)
    return jax.shard_map(
        on_device, mesh=mesh, in_specs=in_specs, out_specs=out_specs, check_vma=False
    )
```

profile of v0, /device:TPU:1, one launch (start us, length us, event | category | flops | bytes accessed | tf_op | source)
XLA Modules:
  0.0 1108.0 jit_solution(15392384441645714204)
XLA Ops:
  0.0 17.9 %copy.69 = bf16[2,32,512,1,256]{4,1,3,0,2:T(8,128)(2,1)} copy(bf16[2,32,512,1,256]{4,2,3,1,0:T(8,128)(2,1)} %param.6) | data formatting | bytes 33554432 | tf_op args[0]
  17.9 7.5 all-to-all-start
  25.4 1.1 dynamic-slice_convert_fusion
  26.7 0.3 copy.75
  27.2 7.0 scatter_fusion
  34.1 0.4 fusion.28
  34.5 288.0 %all-to-all-done = bf16[2,32,512,1,256]{4,1,3,0,2:T(8,128)(2,1)} async-done(((bf16[2,32,512,1,256]{4,1,3,0,2:T(8,128)(2,1)}), bf16[2,32,512,1,256]{4,1,3,0,2:T(8,128)(2,1)}, u32[]{:S(2)}, u32[]{:S(2)}) %all-to-all-start) | async-done | bytes 16777248 | tf_op jit(solution)/shard_map/all_to_all | solution.py:28
  322.5 10.2 copy.70
  332.8 6.4 fusion.27
  339.2 11.5 %copy.73 = bf16[1,16,32,32,1,256]{5,2,1,3,4,0:T(8,128)(2,1)} copy(bf16[1,16,32,32,1,256]{5,3,1,2,0,4:T(8,128)(2,1)} %get-tuple-element.9) | data formatting | bytes 16777216 | tf_op jit(solution)/shard_map/slice | solution.py:30
  350.7 11.7 %fusion.4 = f32[512,32,256]{2,0,1:T(8,128)} fusion(bf16[512,32,256]{2,0,1:T(8,128)(2,1)} %bitcast.91, bf16[2,512,512]{2,1,0:T(8,128)(2,1)S(1)} %copy-done.4), kind=kOutput, calls=%fused_computation.13 | convolution fusion | flops 4294967296 | bytes 25690112 | tf_op jit(solution)/shard_map/abkr,ac->cbkr/dot_general | solution.py:10
  362.3 8.8 fusion.6
  371.2 11.4 %copy.71 = bf16[1,16,32,32,1,256]{5,2,1,3,4,0:T(8,128)(2,1)} copy(bf16[1,16,32,32,1,256]{5,3,1,2,0,4:T(8,128)(2,1)} %get-tuple-element.10) | data formatting | bytes 16777216 | tf_op jit(solution)/shard_map/slice | solution.py:30
  382.5 11.5 %fusion.8 = f32[512,32,256]{2,0,1:T(8,128)} fusion(bf16[512,32,256]{2,0,1:T(8,128)(2,1)} %bitcast.89, bf16[2,512,512]{2,1,0:T(8,128)(2,1)S(1)} %copy-done.4), kind=kOutput, calls=%fused_computation.17 | convolution fusion | flops 4294967296 | bytes 25690112 | tf_op jit(solution)/shard_map/abkr,ac->cbkr/dot_general | solution.py:10
  394.0 26.0 %add_convert_fusion.1 = (bf16[512,32,256]{2,0,1:T(8,128)(2,1)}, bf16[512,32,256]{2,0,1:T(8,128)(2,1)}) fusion(f32[512,32]{0,1:T(8,128)S(1)} %copy.74, f32[512,32]{0,1:T(8,128)S(1)} %copy.67, f32[512,32,256]{2,0,1:T(8,128)} %fusion.6, f32[512,32,256]{2,0,1:T(8,128)} %fusion.8, f32[512,32,256]{2,0,1:T(8,128)} %fusion.4, bf16[512,32,256]{2,0,1:T(8,128)(2,1)} %bitcast.90, ...), kind=kOutput, calls=%fused_computation.7 | convolution fusion | flops 4336910336 | bytes 76152832 | tf_op jit(solution)/shard_map/abkr,ac->cbkr/dot_general | solution.py:10
  420.0 11.6 %fusion.24 = f32[512,32,256]{2,0,1:T(8,128)} fusion(bf16[512,32,256]{2,0,1:T(8,128)(2,1)} %get-tuple-element.6, bf16[1,256,256]{2,0,1:T(2,128)(2,1)S(1)} %get-tuple-element.13), kind=kOutput, calls=%fused_computation.38 | convolution fusion | flops 2147483648 | bytes 25296896 | tf_op jit(solution)/shard_map/abkr,rq->abkq/dot_general | solution.py:10
  431.7 8.5 fusion.25
  440.2 13.7 %fusion = bf16[1,512,32,1,256]{4,1,2,3,0:T(8,128)(2,1)} fusion(f32[512,32,256]{2,0,1:T(8,128)} %fusion.24, bf16[512,32,256]{2,0,1:T(8,128)(2,1)} %get-tuple-element.5, bf16[1,256,256]{2,0,1:T(2,128)(2,1)S(1)} %get-tuple-element.14), kind=kOutput, calls=%fused_computation.9 | convolution fusion | flops 2155872256 | bytes 33685504 | tf_op jit(solution)/shard_map/abkr,rq->abkq/dot_general | solution.py:10
  453.9 13.7 %fusion.1 = bf16[1,512,32,1,256]{4,1,2,3,0:T(8,128)(2,1)} fusion(f32[512,32,256]{2,0,1:T(8,128)} %fusion.25, bf16[512,32,256]{2,0,1:T(8,128)(2,1)} %get-tuple-element.5, bf16[1,256,256]{2,0,1:T(2,128)(2,1)S(1)} %get-tuple-element.13), kind=kOutput, calls=%fused_computation.10 | convolution fusion | flops 2155872256 | bytes 33685504 | tf_op jit(solution)/shard_map/abkr,rq->abkq/dot_general | solution.py:10
  467.7 8.0 pad_maximum_fusion.1
  475.7 23.6 %copy.78 = bf16[2,512,32,1,256]{4,2,3,0,1:T(8,128)(2,1)S(1)} copy(bf16[2,512,32,1,256]{4,1,2,3,0:T(8,128)(2,1)S(1)} %pad_maximum_fusion.1) | data formatting | bytes 33554432 | tf_op jit(solution)/shard_map/stack | solution.py:41
  499.2 432.2 %all_to_all.30 = bf16[2,512,32,1,256]{4,2,3,0,1:T(8,128)(2,1)} all-to-all(bf16[2,512,32,1,256]{4,2,3,0,1:T(8,128)(2,1)S(1)} %copy.78), channel_id=1, replica_groups=mesh['cuts'=2,'inter'=16] {'inter'}, dimensions={1} | all-to-all | bytes 33554432 | tf_op jit(solution)/shard_map/all_to_all | solution.py:42
  931.4 8.2 copy.79
  939.7 6.3 fusion.26
  946.0 8.2 copy.80
  954.2 11.8 %fusion.14 = f32[32,256,512]{2,1,0:T(8,128)} fusion(bf16[32,512,256]{2,1,0:T(8,128)(2,1)} %bitcast.87, bf16[2,512,512]{2,1,0:T(8,128)(2,1)S(1)} %copy-done.3), kind=kOutput, calls=%fused_computation.23 | convolution fusion | flops 4294967296 | bytes 25690112 | tf_op jit(solution)/shard_map/abkr,bc->ackr/dot_general | solution.py:10
  965.9 8.5 fusion.10
  974.5 8.1 copy.82
  982.5 16.3 %subtract_bitcast_fusion = f32[32,512,1,1,256]{1,4,0,3,2:T(8,128)} fusion(f32[32,256,512]{2,1,0:T(8,128)} %fusion.14, bf16[32,512,256]{2,1,0:T(8,128)(2,1)} %bitcast.95, bf16[2,512,512]{2,1,0:T(8,128)(2,1)S(1)} %copy-done.3), kind=kOutput, calls=%fused_computation.4 | convolution fusion | flops 4299161600 | bytes 42467328 | tf_op jit(solution)/shard_map/abkr,bc->ackr/dot_general | solution.py:10
  998.9 12.2 %add_bitcast_fusion = f32[32,512,1,1,256]{1,4,0,3,2:T(8,128)} fusion(f32[32,256,512]{2,1,0:T(8,128)} %fusion.10, bf16[32,512,256]{2,1,0:T(8,128)(2,1)S(1)} %bitcast.96, bf16[2,512,512]{2,1,0:T(8,128)(2,1)S(1)} %copy-done.3), kind=kOutput, calls=%fused_computation.3 | convolution fusion | flops 4299161600 | bytes 42467328 | tf_op jit(solution)/shard_map/abkr,bc->ackr/dot_general | solution.py:10
  1011.1 23.2 %pad_maximum_fusion = f32[32,512,2,1,256]{1,4,0,3,2:T(8,128)} fusion(f32[32,512,1,1,256]{1,4,0,3,2:T(8,128)} %add_bitcast_fusion, f32[32,512,1,1,256]{1,4,0,3,2:T(8,128)} %subtract_bitcast_fusion), kind=kLoop, calls=%fused_computation.1 | loop fusion | flops 8388608 | bytes 67108864 | tf_op jit(solution)/shard_map/stack | solution.py:46
  1034.3 73.5 %copy.86 = f32[32,512,2,1,256]{4,3,2,1,0:T(1,128)} copy(f32[32,512,2,1,256]{1,4,0,3,2:T(8,128)} %pad_maximum_fusion) | data formatting | bytes 67108864 | tf_op jit(solution)/shard_map/stack | solution.py:46
  (24 shorter events, 0.4 us)
Async XLA Ops:
  17.9 8.8 copy-start.5
  17.9 9.1 copy-start.6
  17.9 304.6 %all-to-all-start = ((bf16[2,32,512,1,256]{4,1,3,0,2:T(8,128)(2,1)}), bf16[2,32,512,1,256]{4,1,3,0,2:T(8,128)(2,1)}, u32[]{:S(2)}, u32[]{:S(2)}) async-start(bf16[2,32,512,1,256]{4,1,3,0,2:T(8,128)(2,1)} %copy.69), calls=%async_computation | async-start | bytes 33554432 | tf_op jit(solution)/shard_map/all_to_all | solution.py:28
  339.2 11.5 %copy-start.4 = (bf16[2,512,512]{2,1,0:T(8,128)(2,1)S(1)}, bf16[2,512,512]{2,1,0:T(8,128)(2,1)}, u32[]{:S(2)}) copy-start(bf16[2,512,512]{2,1,0:T(8,128)(2,1)} %param.7) | copy-start | bytes 3145732
  350.7 11.7 %slice-start = ((s8[8388608]{0:T(1024)(128)(4,1)}), s8[4194304]{0:T(1024)(128)(4,1)S(1)}, s32[]{:S(2)}) async-start(s8[8388608]{0:T(1024)(128)(4,1)} %bitcast.92), calls=%async_computation.2 | async-start | bytes 8388608
  350.7 11.7 %slice-start.1 = ((s8[8388608]{0:T(1024)(128)(4,1)}), s8[4194304]{0:T(1024)(128)(4,1)S(1)}, s32[]{:S(2)}) async-start(s8[8388608]{0:T(1024)(128)(4,1)} %bitcast.92), calls=%async_computation.3 | async-start | bytes 8388608
  420.0 11.6 %copy-start = (bf16[512,32,256]{2,0,1:T(8,128)(2,1)S(1)}, bf16[512,32,256]{2,0,1:T(8,128)(2,1)}, u32[]{:S(2)}) copy-start(bf16[512,32,256]{2,0,1:T(8,128)(2,1)} %get-tuple-element.6) | copy-start | bytes 25165828
  946.0 8.2 copy-start.3
  954.2 11.8 %copy-start.1 = (bf16[1,32,16,32,1,256]{5,3,2,1,4,0:T(8,128)(2,1)S(1)}, bf16[1,32,16,32,1,256]{5,3,2,1,4,0:T(8,128)(2,1)}, u32[]{:S(2)}) copy-start(bf16[1,32,16,32,1,256]{5,3,2,1,4,0:T(8,128)(2,1)} %copy.80) | copy-start | bytes 25165828
  982.5 16.3 %copy-start.2 = (bf16[1,32,16,32,1,256]{5,3,2,1,4,0:T(8,128)(2,1)S(1)}, bf16[1,32,16,32,1,256]{5,3,2,1,4,0:T(8,128)(2,1)}, u32[]{:S(2)}) copy-start(bf16[1,32,16,32,1,256]{5,3,2,1,4,0:T(8,128)(2,1)} %copy.82) | copy-start | bytes 25165828
where the time goes:
time: 1120 us; the launch traced here: 1110 us
  blocking collectives  432 us (39%)
  waiting for transfers between devices  288 us (26%)
  local copies, waits for them, and re-layouts  193 us (17%)
  matrix products  154 us (14%)
  other arithmetic  32.3 us (3%)
    all_to_all x1, blocking collectives, on_device(): lax.all_to_all(second, 'inter', split_axis=1, concat_axis=2, tiled=True)  432 us
    all_to_all x1, waiting for transfers between devices, on_device(): lax.all_to_all(stem_tensor, 'inter', split_axis=2, concat_axis=1, tiled=T...  288 us
    dot_general x12, matrix products, product(): jnp.einsum(pattern, first_op, second_op, preferred_element_type=jnp.float32)  154 us
    another operation x1, local copies, waits for them, and re-layouts, on_device(): return jnp.stack([out_real, out_imag], axis=2)  73.5 us
    another operation x1, local copies, waits for them, and re-layouts, on_device(): second = jnp.stack([real_two, imag_two]).astype(jnp.bfloat16)  23.6 us
    another operation x1, other arithmetic, on_device(): return jnp.stack([out_real, out_imag], axis=2)  23.2 us
  transfers between devices with their start and end apart: 1, of which 1 were waited for; matrix products, arithmetic and copies ran while one was open for 1% of the time, Pallas kernels for 0%

commit v1 on v0

--- a/solution.py
+++ b/solution.py
@@ -1,7 +1,14 @@
+import functools
+
 import jax
 import jax.numpy as jnp
 from jax import lax
+from jax.experimental import pallas as pl
+from jax.experimental.pallas import tpu as pltpu
 from jax.sharding import PartitionSpec as P
+
+MESH = pl.DeviceIdType.MESH
+CHUNKS = 2
 
 
 def complex_mix(input_real, input_imag, weight_real, weight_imag, pattern):
@@ -15,7 +22,7 @@
     )
 
 
-def on_device(stem_tensor, branch_one, branch_two, mode_order, branch_three, closing):
+def plain_device(stem_tensor, branch_one, branch_two, mode_order, branch_three, closing):
     group_size = lax.axis_size("inter")
     my_index = lax.axis_index("inter")
     local_b = branch_three.shape[1] // group_size
@@ -46,6 +53,302 @@
     return jnp.stack([out_real, out_imag], axis=2)
 
 
+def swap_kernel(
+    n, stem, w_one, w_two, close_ref, to_b, to_a, returned,
+    held, turned, out_send, out_recv, back_send, back_recv, own_sem,
+):
+    me = lax.axis_index("inter")
+    la = stem.shape[1]
+    chunks, _, size_a, cb, size_r = held.shape
+    lb = chunks * cb
+
+    def rows(d):
+        return pl.ds(pl.multiple_of(d * la, la), la)
+
+    def peer(i):
+        return lax.rem(me + i, n)
+
+    def away(k, i):
+        d = peer(i)
+        return pltpu.make_async_remote_copy(
+            src_ref=stem.at[:, :, pl.ds(pl.multiple_of(d * lb + k * cb, cb), cb), :],
+            dst_ref=held.at[k, :, rows(me)],
+            send_sem=out_send.at[k, i],
+            recv_sem=out_recv.at[k, me],
+            device_id={"inter": d},
+            device_id_type=MESH,
+        )
+
+    def arrival(k, s):
+        return pltpu.make_async_remote_copy(
+            src_ref=stem.at[:, :, pl.ds(k * cb, cb), :],
+            dst_ref=held.at[k, :, rows(s)],
+            send_sem=out_send.at[k, 0],
+            recv_sem=out_recv.at[k, s],
+            device_id={"inter": s},
+            device_id_type=MESH,
+        )
+
+    def own_in(k):
+        return pltpu.make_async_copy(
+            stem.at[:, :, pl.ds(pl.multiple_of(me * lb + k * cb, cb), cb), :],
+            held.at[k, :, rows(me)],
+            own_sem.at[0, k],
+        )
+
+    def back(k, i):
+        d = peer(i)
+        return pltpu.make_async_remote_copy(
+            src_ref=held.at[k, :, rows(d)],
+            dst_ref=returned.at[:, :, pl.ds(pl.multiple_of(me * lb + k * cb, cb), cb), :],
+            send_sem=back_send.at[k, i],
+            recv_sem=back_recv.at[k, me],
+            device_id={"inter": d},
+            device_id_type=MESH,
+        )
+
+    def back_arrival(k, s):
+        return pltpu.make_async_remote_copy(
+            src_ref=held.at[k, :, rows(s)],
+            dst_ref=returned.at[:, :, pl.ds(pl.multiple_of(s * lb + k * cb, cb), cb), :],
+            send_sem=back_send.at[k, 0],
+            recv_sem=back_recv.at[k, s],
+            device_id={"inter": s},
+            device_id_type=MESH,
+        )
+
+    def own_back(k):
+        return pltpu.make_async_copy(
+            held.at[k, :, rows(me)],
+            returned.at[:, :, pl.ds(pl.multiple_of(me * lb + k * cb, cb), cb), :],
+            own_sem.at[1, k],
+        )
+
+    barrier = pltpu.get_barrier_semaphore()
+
+    @pl.loop(1, n)
+    def _(i):
+        pl.semaphore_signal(barrier, inc=1, device_id={"inter": peer(i)}, device_id_type=MESH)
+
+    pl.semaphore_wait(barrier, n - 1)
+
+    @pl.loop(1, n)
+    def _(i):
+        away(0, i).start()
+
+    for k in range(chunks):
+        own_in(k).start()
+
+    for k in range(1, chunks):
+        @pl.loop(1, n)
+        def _(i):
+            away(k - 1, i).wait_send()
+            away(k, i).start()
+
+    for k in range(chunks):
+        own_in(k).wait()
+
+        def turn(s):
+            for p in range(2):
+                block = held[k, p, rows(s)].reshape(la * cb, size_r)
+                moved = jnp.dot(to_b[...], block, preferred_element_type=jnp.float32)
+                turned[:, pl.ds(pl.multiple_of(p * size_a + s * la, la), la), :] = (
+                    moved.astype(jnp.bfloat16).reshape(cb, la, size_r)
+                )
+
+        turn(me)
+
+        @pl.loop(1, n)
+        def _(i):
+            s = peer(i)
+            arrival(k, s).wait_recv()
+            turn(s)
+
+        @pl.loop(0, cb)
+        def _(b):
+            mixed = jnp.dot(w_one[...], turned[b], preferred_element_type=jnp.float32)
+            hot = lax.broadcasted_iota(jnp.int32, (close_ref.shape[1], size_r), 0) == k * cb + b
+            gate = jnp.dot(
+                close_ref[...],
+                jnp.where(hot, 1.0, 0.0).astype(jnp.bfloat16),
+                preferred_element_type=jnp.float32,
+            )
+            real_part, imag_part = mixed[:size_a], mixed[size_a:]
+            gate_real, gate_imag = gate[:size_a], gate[size_a:]
+            phased = jnp.concatenate(
+                [
+                    (gate_real * real_part - gate_imag * imag_part).astype(jnp.bfloat16),
+                    (gate_real * imag_part + gate_imag * real_part).astype(jnp.bfloat16),
+                ],
+                axis=1,
+            )
+            both = jnp.dot(phased, w_two[...], preferred_element_type=jnp.float32).astype(
+                jnp.bfloat16
+            )
+            turned[b, :size_a] = both[:, :size_r]
+            turned[b, size_a:] = both[:, size_r:]
+
+        def unturn(d):
+            for p in range(2):
+                block = turned[
+                    :, pl.ds(pl.multiple_of(p * size_a + d * la, la), la), :
+                ].reshape(cb * la, size_r)
+                moved = jnp.dot(to_a[...], block, preferred_element_type=jnp.float32)
+                held[k, p, rows(d)] = moved.astype(jnp.bfloat16).reshape(la, cb, size_r)
+
+        @pl.loop(1, n)
+        def _(i):
+            unturn(peer(i))
+            back(k, i).start()
+
+        unturn(me)
+        own_back(k).start()
+
+    @pl.loop(1, n)
+    def _(i):
+        away(chunks - 1, i).wait_send()
+
+    for k in range(chunks):
+        own_back(k).wait()
+
+        @pl.loop(1, n)
+        def _(i):
+            back(k, i).wait_send()
+            back_arrival(k, peer(i)).wait_recv()
+
+
+def close_kernel(block_ref, w_three, out_ref):
+    two, _, size_b, size_q = block_ref.shape
+    half = size_q // 2
+    block = block_ref[:, 0].reshape(two * size_b, size_q)
+    mixed = jnp.dot(w_three[...], block, preferred_element_type=jnp.float32)
+    groups = mixed.shape[0] // 8
+    left = mixed[:, :half].reshape(groups, 8, half)
+    right = mixed[:, half:].reshape(groups, 8, half)
+    even = lax.broadcasted_iota(jnp.int32, left.shape, 1) % 2 == 0
+    low = jnp.where(even, left, pltpu.roll(right, 1, 1))
+    high = jnp.where(even, pltpu.roll(left, 7, 1), right)
+    out_ref[:, 0] = low
+    out_ref[:, 1] = high
+
+
+def kernel_device(stem_tensor, branch_one, branch_two, mode_order, branch_three, closing):
+    n = lax.axis_size("inter")
+    me = lax.axis_index("inter")
+    _, la, size_b, _, size_r = stem_tensor.shape
+    size_a = branch_one.shape[1]
+    size_c = branch_three.shape[2]
+    lb = size_b // n
+    cb = lb // CHUNKS
+    stem = stem_tensor.reshape(2, la, size_b, size_r)
+
+    one_t = jnp.swapaxes(branch_one, 1, 2)
+    w_one = jnp.concatenate(
+        [
+            jnp.concatenate([one_t[0], -one_t[1]], axis=1),
+            jnp.concatenate([one_t[1], one_t[0]], axis=1),
+        ],
+        axis=0,
+    )
+    places = (jnp.arange(size_r, dtype=jnp.int32)[:, None] == mode_order[None, :]).astype(
+        jnp.bfloat16
+    )
+    permuted = jnp.einsum(
+        "ir,prq->piq", places, branch_two, preferred_element_type=jnp.float32
+    ).astype(jnp.bfloat16)
+    w_two = jnp.concatenate(
+        [
+            jnp.concatenate([permuted[0], permuted[1]], axis=1),
+            jnp.concatenate([-permuted[1], permuted[0]], axis=1),
+        ],
+        axis=0,
+    )
+    close_cols = lax.dynamic_slice_in_dim(closing, me * lb, lb, 2).reshape(2 * size_a, lb)
+    close_cols = jnp.pad(close_cols, ((0, 0), (0, -lb % 128)))
+    line = jnp.arange(la * cb, dtype=jnp.int32)
+    to_b = ((line // la)[:, None] == (line % cb)[None, :]) & (
+        (line % la)[:, None] == (line // cb)[None, :]
+    )
+    to_b = to_b.astype(jnp.bfloat16)
+    to_a = to_b.T
+
+    vmem = pl.BlockSpec(memory_space=pltpu.VMEM)
+    anywhere = pl.BlockSpec(memory_space=pl.ANY)
+    returned = pl.pallas_call(
+        functools.partial(swap_kernel, n),
+        out_shape=jax.ShapeDtypeStruct((2, la, size_b, size_r), jnp.bfloat16),
+        in_specs=[anywhere, vmem, vmem, vmem, vmem, vmem],
+        out_specs=anywhere,
+        scratch_shapes=[
+            pltpu.VMEM((CHUNKS, 2, size_a, cb, size_r), jnp.bfloat16),
+            pltpu.VMEM((cb, 2 * size_a, size_r), jnp.bfloat16),
+            pltpu.SemaphoreType.DMA((CHUNKS, n)),
+            pltpu.SemaphoreType.DMA((CHUNKS, n)),
+            pltpu.SemaphoreType.DMA((CHUNKS, n)),
+            pltpu.SemaphoreType.DMA((CHUNKS, n)),
+            pltpu.SemaphoreType.DMA((2, CHUNKS)),
+        ],
+        compiler_params=pltpu.CompilerParams(
+            collective_id=0, has_side_effects=True, vmem_limit_bytes=52 * 1024 * 1024
+        ),
+        cost_estimate=pl.CostEstimate(
+            flops=24 * size_a * size_a * lb * size_r,
+            bytes_accessed=16 * size_a * lb * size_r,
+            transcendentals=0,
+        ),
+    )(stem, w_one, w_two, close_cols, to_b, to_a)
+
+    three_t = jnp.swapaxes(branch_three, 1, 2)
+    w_three = jnp.stack(
+        [
+            jnp.concatenate([three_t[0], -three_t[1]], axis=1),
+            jnp.concatenate([three_t[1], three_t[0]], axis=1),
+        ],
+        axis=1,
+    )
+    w_three = (
+        w_three.reshape(size_c // 4, 2, 2, 2, 2 * size_b)
+        .transpose(0, 2, 3, 1, 4)
+        .reshape(2 * size_c, 2 * size_b)
+    )
+    groups = size_c // 4
+    half = size_r // 2
+    out = pl.pallas_call(
+        close_kernel,
+        grid=(la,),
+        out_shape=jax.ShapeDtypeStruct((la * groups, 2, 8, half), jnp.float32),
+        in_specs=[
+            pl.BlockSpec((2, 1, size_b, size_r), lambda a: (0, a, 0, 0)),
+            pl.BlockSpec((2 * size_c, 2 * size_b), lambda a: (0, 0)),
+        ],
+        out_specs=pl.BlockSpec((groups, 2, 8, half), lambda a: (a, 0, 0, 0)),
+        compiler_params=pltpu.CompilerParams(vmem_limit_bytes=56 * 1024 * 1024),
+        cost_estimate=pl.CostEstimate(
+            flops=8 * la * size_b * size_c * size_r,
+            bytes_accessed=la * (4 * size_b + 8 * size_c) * size_r,
+            transcendentals=0,
+        ),
+    )(returned, w_three)
+    return out.reshape(la, size_c, 2, 1, size_r)
+
+
+def on_device(stem_tensor, branch_one, branch_two, mode_order, branch_three, closing):
+    n = lax.axis_size("inter")
+    _, la, size_b, amps, size_r = stem_tensor.shape
+    lb = size_b // n
+    fits = (
+        amps == 1
+        and n > 1
+        and la % 16 == 0
+        and lb % (16 * CHUNKS) == 0
+        and size_r == 256
+        and branch_one.shape[1] % 16 == 0
+        and branch_three.shape[2] % 4 == 0
+    )
+    device = kernel_device if fits else plain_device
+    return device(stem_tensor, branch_one, branch_two, mode_order, branch_three, closing)
+
+
 def solution(mesh):
     in_specs = (P(None, ("cuts", "inter"), None, None, None), P(), P(), P(), P(), P())
     out_specs = P(("cuts", "inter"), None, None, None, None)

time: 1120 us -> 807 us (0.72)
  the two profiles are of different devices: /device:TPU:1 before, /device:TPU:27 now
where the time goes in v1:
time: 807 us; the launch traced here: 806 us
  Pallas kernels  782 us (97%)
  local copies, waits for them, and re-layouts  16.4 us (2%)
    pallas_call x1, Pallas kernels, kernel_device(): pl.pallas_call(functools.partial(swap_kernel, n), out_shape=jax.ShapeDtyp...  745 us
    pallas_call x1, Pallas kernels, kernel_device(): pl.pallas_call(close_kernel, grid=(la,), out_shape=jax.ShapeDtypeStruct((...  36.9 us

profile of v1, /device:TPU:27, one launch (start us, length us, event | category | flops | bytes accessed | tf_op | source)
XLA Modules:
  0.0 805.6 jit_solution(814780343512336939)
XLA Ops:
  0.0 0.0 copy-start
  0.0 1.2 copy-done
  1.2 0.1 constant_dynamic-slice_fusion
  1.4 0.1 pad.4.close_ref
  1.4 1.2 fusion
  2.7 0.5 and_convert_fusion
  3.3 1.5 copy.15
  4.8 0.0 copy-start.2
  4.8 0.1 slice_bitcast_fusion
  4.9 1.6 maximum_maximum_fusion.w_one
  6.6 0.0 copy-done.2
  6.6 0.9 fusion.15
  7.4 0.2 copy.19
  7.7 0.2 squeeze.26
  7.9 0.5 neg.16
  8.3 2.1 copy.18
  10.4 2.0 concatenate.35
  12.4 3.5 maximum_bitcast_fusion
  16.0 3.9 copy.20
  19.9 4.1 reshape.78.w_three
  24.0 744.7 %shard_map.64.block_ref = bf16[2,32,512,256]{3,2,1,0:T(8,128)(2,1)} custom-call(bf16[2,32,512,256]{3,2,1,0:T(8,128)(2,1)} %bitcast.29, bf16[1024,1024]{1,0:T(8,128)(2,1)} %maximum_maximum_fusion.w_one, bf16[512,512]{1,0:T(8,128)(2,1)S(1)} %maximum_maximum_fusion.1.w_two, bf16[1024,128]{1,0:T(8,128)(2,1)S(1)} %pad.4.close_ref, ...), custom_call_target="tpu_custom_call" | custom-call | flops 51539607552 | bytes 67108864 | tf_op jit(solution)/shard_map/pallas_call | solution.py:277
  768.7 0.0 copy-start.1
  768.7 36.9 %shard_map.65 = f32[4096,2,8,128]{3,2,1,0:T(8,128)} custom-call(bf16[2,32,512,256]{3,2,1,0:T(8,128)(2,1)} %shard_map.64.block_ref, bf16[1024,1024]{1,0:T(8,128)(2,1)} %reshape.78.w_three), custom_call_target="tpu_custom_call" | custom-call | flops 17179869184 | bytes 50331648 | tf_op jit(solution)/shard_map/pallas_call | solution.py:316
  805.6 0.0 copy-done.1
  (6 shorter events, 0.1 us)
Async XLA Ops:
  0.0 1.2 copy-start
  4.8 1.8 copy-start.2
  768.7 36.9 %copy-start.1 = (bf16[2,512,512]{2,1,0:T(8,128)(2,1)S(1)}, bf16[2,512,512]{2,1,0:T(8,128)(2,1)}, u32[]{:S(2)}) copy-start(bf16[2,512,512]{2,1,0:T(8,128)(2,1)} %param.11) | copy-start | bytes 3145732

commit v2 on v1

--- a/solution.py
+++ b/solution.py
@@ -2,6 +2,7 @@
 
 import jax
 import jax.numpy as jnp
+import numpy as np
 from jax import lax
 from jax.experimental import pallas as pl
 from jax.experimental.pallas import tpu as pltpu
@@ -9,6 +10,7 @@
 
 MESH = pl.DeviceIdType.MESH
 CHUNKS = 2
+RUN = 64
 
 
 def complex_mix(input_real, input_imag, weight_real, weight_imag, pattern):
@@ -54,24 +56,30 @@
 
 
 def swap_kernel(
-    n, stem, w_one, w_two, close_ref, to_b, to_a, returned,
-    held, turned, out_send, out_recv, back_send, back_recv, own_sem,
+    n, stem, branch_one, branch_two, mode_order, branch_three, closing, to_b, to_a, spread,
+    returned, w_three,
+    held, turned, w_one, w_two, close_ref, stacked, shuffled,
+    out_send, out_recv, back_send, back_recv, own_sem,
 ):
     me = lax.axis_index("inter")
     la = stem.shape[1]
     chunks, _, size_a, cb, size_r = held.shape
     lb = chunks * cb
+    stride = 7 if n % 7 else 1
 
     def rows(d):
         return pl.ds(pl.multiple_of(d * la, la), la)
 
     def peer(i):
-        return lax.rem(me + i, n)
+        return lax.rem(me + stride * i, n)
+
+    def columns(d, k):
+        return pl.ds(pl.multiple_of(d * lb + k * cb, cb), cb)
 
     def away(k, i):
         d = peer(i)
         return pltpu.make_async_remote_copy(
-            src_ref=stem.at[:, :, pl.ds(pl.multiple_of(d * lb + k * cb, cb), cb), :],
+            src_ref=stem.at[:, :, columns(d, k), :],
             dst_ref=held.at[k, :, rows(me)],
             send_sem=out_send.at[k, i],
             recv_sem=out_recv.at[k, me],
@@ -81,7 +89,7 @@
 
     def arrival(k, s):
         return pltpu.make_async_remote_copy(
-            src_ref=stem.at[:, :, pl.ds(k * cb, cb), :],
+            src_ref=stem.at[:, :, columns(0, k), :],
             dst_ref=held.at[k, :, rows(s)],
             send_sem=out_send.at[k, 0],
             recv_sem=out_recv.at[k, s],
@@ -91,16 +99,14 @@
 
     def own_in(k):
         return pltpu.make_async_copy(
-            stem.at[:, :, pl.ds(pl.multiple_of(me * lb + k * cb, cb), cb), :],
-            held.at[k, :, rows(me)],
-            own_sem.at[0, k],
+            stem.at[:, :, columns(me, k), :], held.at[k, :, rows(me)], own_sem.at[0, k]
         )
 
     def back(k, i):
         d = peer(i)
         return pltpu.make_async_remote_copy(
             src_ref=held.at[k, :, rows(d)],
-            dst_ref=returned.at[:, :, pl.ds(pl.multiple_of(me * lb + k * cb, cb), cb), :],
+            dst_ref=returned.at[k, me],
             send_sem=back_send.at[k, i],
             recv_sem=back_recv.at[k, me],
             device_id={"inter": d},
@@ -110,7 +116,7 @@
     def back_arrival(k, s):
         return pltpu.make_async_remote_copy(
             src_ref=held.at[k, :, rows(s)],
-            dst_ref=returned.at[:, :, pl.ds(pl.multiple_of(s * lb + k * cb, cb), cb), :],
+            dst_ref=returned.at[k, s],
             send_sem=back_send.at[k, 0],
             recv_sem=back_recv.at[k, s],
             device_id={"inter": s},
@@ -119,10 +125,11 @@
 
     def own_back(k):
         return pltpu.make_async_copy(
-            held.at[k, :, rows(me)],
-            returned.at[:, :, pl.ds(pl.multiple_of(me * lb + k * cb, cb), cb), :],
-            own_sem.at[1, k],
-        )
+            held.at[k, :, rows(me)], returned.at[k, me], own_sem.at[1, k]
+        )
+
+    def weights_out():
+        return pltpu.make_async_copy(shuffled, w_three, own_sem.at[2, 0])
 
     barrier = pltpu.get_barrier_semaphore()
 
@@ -138,6 +145,54 @@
 
     for k in range(chunks):
         own_in(k).start()
+
+    one_real = branch_one[0].astype(jnp.float32).T.astype(jnp.bfloat16)
+    one_imag = branch_one[1].astype(jnp.float32).T.astype(jnp.bfloat16)
+    w_one[:size_a, :size_a] = one_real
+    w_one[:size_a, size_a:] = -one_imag
+    w_one[size_a:, :size_a] = one_imag
+    w_one[size_a:, size_a:] = one_real
+
+    hot = lax.broadcasted_iota(jnp.int32, (size_r, size_r), 0) == mode_order[...]
+    places = jnp.where(hot, 1.0, 0.0).astype(jnp.bfloat16)
+    two_real = jnp.dot(places, branch_two[0], preferred_element_type=jnp.float32)
+    two_imag = jnp.dot(places, branch_two[1], preferred_element_type=jnp.float32)
+    w_two[:size_r, :size_r] = two_real.astype(jnp.bfloat16)
+    w_two[:size_r, size_r:] = two_imag.astype(jnp.bfloat16)
+    w_two[size_r:, :size_r] = (-two_imag).astype(jnp.bfloat16)
+    w_two[size_r:, size_r:] = two_real.astype(jnp.bfloat16)
+
+    pick = (closing.shape[2], close_ref.shape[1])
+    picked = lax.broadcasted_iota(jnp.int32, pick, 0) == (
+        lax.broadcasted_iota(jnp.int32, pick, 1) + me * lb
+    )
+    picked = jnp.where(picked, 1.0, 0.0).astype(jnp.bfloat16)
+    for p in range(2):
+        close_ref[p * size_a : (p + 1) * size_a] = jnp.dot(
+            closing[p], picked, preferred_element_type=jnp.float32
+        ).astype(jnp.bfloat16)
+
+    width = 2 * n * cb
+    for k in range(chunks):
+        for part in range(2):
+            pieces = []
+            for s in range(n):
+                piece = branch_three[:, s * lb + k * cb : s * lb + (k + 1) * cb, :].astype(
+                    jnp.float32
+                )
+                pieces += [piece[0], -piece[1]] if part == 0 else [piece[1], piece[0]]
+            stacked[part, :, k * width : (k + 1) * width] = (
+                jnp.concatenate(pieces, axis=0).T.astype(jnp.bfloat16)
+            )
+    run = spread.shape[0] // 2
+    for t in range(stacked.shape[1] // run):
+        block = jnp.concatenate(
+            [stacked[0, t * run : (t + 1) * run], stacked[1, t * run : (t + 1) * run]], axis=0
+        )
+        shuffled[2 * t * run : 2 * (t + 1) * run] = jnp.dot(
+            spread[...], block, preferred_element_type=jnp.float32
+        ).astype(jnp.bfloat16)
+    weights_out().start()
 
     for k in range(1, chunks):
         @pl.loop(1, n)
@@ -160,7 +215,7 @@
 
         @pl.loop(1, n)
         def _(i):
-            s = peer(i)
+            s = peer(n - i)
             arrival(k, s).wait_recv()
             turn(s)
 
@@ -199,42 +254,40 @@
         @pl.loop(1, n)
         def _(i):
             unturn(peer(i))
+            if k + 1 < chunks:
+                away(k + 1, i).wait_send()
             back(k, i).start()
 
         unturn(me)
         own_back(k).start()
 
-    @pl.loop(1, n)
-    def _(i):
-        away(chunks - 1, i).wait_send()
-
+    weights_out().wait()
     for k in range(chunks):
         own_back(k).wait()
 
         @pl.loop(1, n)
         def _(i):
             back(k, i).wait_send()
-            back_arrival(k, peer(i)).wait_recv()
+            back_arrival(k, peer(n - i)).wait_recv()
 
 
 def close_kernel(block_ref, w_three, out_ref):
-    two, _, size_b, size_q = block_ref.shape
+    chunks, n, two, steps, cb, size_q = block_ref.shape
     half = size_q // 2
-    block = block_ref[:, 0].reshape(two * size_b, size_q)
-    mixed = jnp.dot(w_three[...], block, preferred_element_type=jnp.float32)
-    groups = mixed.shape[0] // 8
-    left = mixed[:, :half].reshape(groups, 8, half)
-    right = mixed[:, half:].reshape(groups, 8, half)
-    even = lax.broadcasted_iota(jnp.int32, left.shape, 1) % 2 == 0
-    low = jnp.where(even, left, pltpu.roll(right, 1, 1))
-    high = jnp.where(even, pltpu.roll(left, 7, 1), right)
-    out_ref[:, 0] = low
-    out_ref[:, 1] = high
+    groups = out_ref.shape[0] // steps
+    for a in range(steps):
+        block = block_ref[:, :, :, a].reshape(chunks * n * two * cb, size_q)
+        mixed = jnp.dot(w_three[...], block, preferred_element_type=jnp.float32)
+        left = mixed[:, :half].reshape(groups, 8, half)
+        right = mixed[:, half:].reshape(groups, 8, half)
+        even = lax.broadcasted_iota(jnp.int32, left.shape, 1) % 2 == 0
+        own = pl.ds(a * groups, groups)
+        out_ref[own, 0] = jnp.where(even, left, pltpu.roll(right, 1, 1))
+        out_ref[own, 1] = jnp.where(even, pltpu.roll(left, 7, 1), right)
 
 
 def kernel_device(stem_tensor, branch_one, branch_two, mode_order, branch_three, closing):
     n = lax.axis_size("inter")
-    me = lax.axis_index("inter")
     _, la, size_b, _, size_r = stem_tensor.shape
     size_a = branch_one.shape[1]
     size_c = branch_three.shape[2]
@@ -242,86 +295,65 @@
     cb = lb // CHUNKS
     stem = stem_tensor.reshape(2, la, size_b, size_r)
 
-    one_t = jnp.swapaxes(branch_one, 1, 2)
-    w_one = jnp.concatenate(
-        [
-            jnp.concatenate([one_t[0], -one_t[1]], axis=1),
-            jnp.concatenate([one_t[1], one_t[0]], axis=1),
-        ],
-        axis=0,
-    )
-    places = (jnp.arange(size_r, dtype=jnp.int32)[:, None] == mode_order[None, :]).astype(
-        jnp.bfloat16
-    )
-    permuted = jnp.einsum(
-        "ir,prq->piq", places, branch_two, preferred_element_type=jnp.float32
-    ).astype(jnp.bfloat16)
-    w_two = jnp.concatenate(
-        [
-            jnp.concatenate([permuted[0], permuted[1]], axis=1),
-            jnp.concatenate([-permuted[1], permuted[0]], axis=1),
-        ],
-        axis=0,
-    )
-    close_cols = lax.dynamic_slice_in_dim(closing, me * lb, lb, 2).reshape(2 * size_a, lb)
-    close_cols = jnp.pad(close_cols, ((0, 0), (0, -lb % 128)))
-    line = jnp.arange(la * cb, dtype=jnp.int32)
-    to_b = ((line // la)[:, None] == (line % cb)[None, :]) & (
-        (line % la)[:, None] == (line // cb)[None, :]
-    )
-    to_b = to_b.astype(jnp.bfloat16)
-    to_a = to_b.T
+    line = np.arange(la * cb)
+    to_b = (
+        ((line // la)[:, None] == (line % cb)[None, :])
+        & ((line % la)[:, None] == (line // cb)[None, :])
+    ).astype(np.float32)
+    g, low, part, high = np.unravel_index(np.arange(2 * RUN), (RUN // 4, 2, 2, 2))
+    spread = np.zeros((2 * RUN, 2 * RUN), np.float32)
+    spread[np.arange(2 * RUN), part * RUN + 4 * g + 2 * high + low] = 1.0
+    to_b, to_a, spread = (jnp.asarray(x, jnp.bfloat16) for x in (to_b, to_b.T, spread))
 
     vmem = pl.BlockSpec(memory_space=pltpu.VMEM)
     anywhere = pl.BlockSpec(memory_space=pl.ANY)
-    returned = pl.pallas_call(
+    returned, w_three = pl.pallas_call(
         functools.partial(swap_kernel, n),
-        out_shape=jax.ShapeDtypeStruct((2, la, size_b, size_r), jnp.bfloat16),
-        in_specs=[anywhere, vmem, vmem, vmem, vmem, vmem],
-        out_specs=anywhere,
+        out_shape=[
+            jax.ShapeDtypeStruct((CHUNKS, n, 2, la, cb, size_r), jnp.bfloat16),
+            jax.ShapeDtypeStruct((2 * size_c, 2 * size_b), jnp.bfloat16),
+        ],
+        in_specs=[anywhere] + [vmem] * 8,
+        out_specs=[anywhere, anywhere],
         scratch_shapes=[
             pltpu.VMEM((CHUNKS, 2, size_a, cb, size_r), jnp.bfloat16),
             pltpu.VMEM((cb, 2 * size_a, size_r), jnp.bfloat16),
+            pltpu.VMEM((2 * size_a, 2 * size_a), jnp.bfloat16),
+            pltpu.VMEM((2 * size_r, 2 * size_r), jnp.bfloat16),
+            pltpu.VMEM((2 * size_a, pl.cdiv(lb, 128) * 128), jnp.bfloat16),
+            pltpu.VMEM((2, size_c, 2 * size_b), jnp.bfloat16),
+            pltpu.VMEM((2 * size_c, 2 * size_b), jnp.bfloat16),
             pltpu.SemaphoreType.DMA((CHUNKS, n)),
             pltpu.SemaphoreType.DMA((CHUNKS, n)),
             pltpu.SemaphoreType.DMA((CHUNKS, n)),
             pltpu.SemaphoreType.DMA((CHUNKS, n)),
-            pltpu.SemaphoreType.DMA((2, CHUNKS)),
+            pltpu.SemaphoreType.DMA((3, CHUNKS)),
         ],
         compiler_params=pltpu.CompilerParams(
-            collective_id=0, has_side_effects=True, vmem_limit_bytes=52 * 1024 * 1024
+            collective_id=0, has_side_effects=True, vmem_limit_bytes=56 * 1024 * 1024
         ),
         cost_estimate=pl.CostEstimate(
             flops=24 * size_a * size_a * lb * size_r,
             bytes_accessed=16 * size_a * lb * size_r,
             transcendentals=0,
         ),
-    )(stem, w_one, w_two, close_cols, to_b, to_a)
-
-    three_t = jnp.swapaxes(branch_three, 1, 2)
-    w_three = jnp.stack(
-        [
-            jnp.concatenate([three_t[0], -three_t[1]], axis=1),
-            jnp.concatenate([three_t[1], three_t[0]], axis=1),
-        ],
-        axis=1,
-    )
-    w_three = (
-        w_three.reshape(size_c // 4, 2, 2, 2, 2 * size_b)
-        .transpose(0, 2, 3, 1, 4)
-        .reshape(2 * size_c, 2 * size_b)
-    )
+    )(
+        stem, branch_one, branch_two, mode_order.reshape(1, size_r), branch_three, closing,
+        to_b, to_a, spread,
+    )
+
     groups = size_c // 4
     half = size_r // 2
+    steps = 4
     out = pl.pallas_call(
         close_kernel,
-        grid=(la,),
+        grid=(la // steps,),
         out_shape=jax.ShapeDtypeStruct((la * groups, 2, 8, half), jnp.float32),
         in_specs=[
-            pl.BlockSpec((2, 1, size_b, size_r), lambda a: (0, a, 0, 0)),
+            pl.BlockSpec((CHUNKS, n, 2, steps, cb, size_r), lambda a: (0, 0, 0, a, 0, 0)),
             pl.BlockSpec((2 * size_c, 2 * size_b), lambda a: (0, 0)),
         ],
-        out_specs=pl.BlockSpec((groups, 2, 8, half), lambda a: (a, 0, 0, 0)),
+        out_specs=pl.BlockSpec((steps * groups, 2, 8, half), lambda a: (a, 0, 0, 0)),
         compiler_params=pltpu.CompilerParams(vmem_limit_bytes=56 * 1024 * 1024),
         cost_estimate=pl.CostEstimate(
             flops=8 * la * size_b * size_c * size_r,
@@ -343,7 +375,7 @@
         and lb % (16 * CHUNKS) == 0
         and size_r == 256
         and branch_one.shape[1] % 16 == 0
-        and branch_three.shape[2] % 4 == 0
+        and branch_three.shape[2] % RUN == 0
     )
     device = kernel_device if fits else plain_device
     return device(stem_tensor, branch_one, branch_two, mode_order, branch_three, closing)

time: 807 us -> 758 us (0.939)
  the two profiles are of different devices: /device:TPU:27 before, /device:TPU:1 now
where the time goes in v2:
time: 758 us
  Pallas kernels  758 us (100%)
    pallas_call x1, Pallas kernels, kernel_device(): pl.pallas_call(functools.partial(swap_kernel, n), out_shape=[jax.ShapeDty...  732 us
    pallas_call x1, Pallas kernels, kernel_device(): pl.pallas_call(close_kernel, grid=(la // steps,), out_shape=jax.ShapeDtyp...  25.8 us

profile of v2, /device:TPU:1, one launch (start us, length us, event | category | flops | bytes accessed | tf_op | source)
XLA Modules:
  0.0 757.8 jit_solution(10780736285073477573)
XLA Ops:
  0.0 732.0 %shard_map.91 = (bf16[2,16,2,32,16,256]{5,4,3,2,1,0:T(8,128)(2,1)}, bf16[1024,1024]{1,0:T(8,128)(2,1)}) custom-call(bf16[2,32,512,256]{3,2,1,0:T(8,128)(2,1)} %bitcast.3, bf16[2,512,512]{2,1,0:T(8,128)(2,1)} %branch_one.1, bf16[2,256,256]{2,1,0:T(8,128)(2,1)} %branch_two.1, s32[1,256]{1,0:T(1,128)} %bitcast.4, bf16[2,512,512]{2,1,0:T(8,128)(2,1)} %branch_three.1, ...), custom_call_target="tpu_custom_call" | custom-call | flops 51539607552 | bytes 67108864 | tf_op jit(solution)/shard_map/pallas_call | solution.py:310
  732.0 25.8 %shard_map.92 = f32[4096,2,8,128]{3,2,1,0:T(8,128)} custom-call(bf16[2,16,2,32,16,256]{5,4,3,2,1,0:T(8,128)(2,1)} %get-tuple-element.7.block_ref, bf16[1024,1024]{1,0:T(8,128)(2,1)} %get-tuple-element.8.w_three), custom_call_target="tpu_custom_call" | custom-call | flops 17179869184 | bytes 50331648 | tf_op jit(solution)/shard_map/pallas_call | solution.py:348

commit v3 on v2

--- a/solution.py
+++ b/solution.py
@@ -58,20 +58,29 @@
 def swap_kernel(
     n, stem, branch_one, branch_two, mode_order, branch_three, closing, to_b, to_a, spread,
     returned, w_three,
-    held, turned, w_one, w_two, close_ref, stacked, shuffled,
-    out_send, out_recv, back_send, back_recv, own_sem,
+    staged, held, turned, w_one, w_two, close_ref, stacked, shuffled,
+    stage_sem, out_send, out_recv, back_send, back_recv, own_sem,
 ):
     me = lax.axis_index("inter")
     la = stem.shape[1]
     chunks, _, size_a, cb, size_r = held.shape
     lb = chunks * cb
-    stride = 7 if n % 7 else 1
+    wing = n // 2
+    base = me // wing * wing
+    other = wing - base
 
     def rows(d):
         return pl.ds(pl.multiple_of(d * la, la), la)
 
     def peer(i):
-        return lax.rem(me + stride * i, n)
+        odd = lax.rem(me, 2)
+        turn_odd = lax.rem(i, 2)
+        last = jnp.where(i == n - 1, 1, 0)
+        crossing = jnp.where(odd == 1, jnp.where(turn_odd == 1, last, 1), turn_odd)
+        step_even = (i - crossing) // 2
+        step_odd = jnp.where(last == 1, wing - 1, (i + 1) // 2 - crossing)
+        step = jnp.where(odd == 1, step_odd, step_even)
+        return jnp.where(crossing == 1, other, base) + lax.rem(me + step, wing)
 
     def columns(d, k):
         return pl.ds(pl.multiple_of(d * lb + k * cb, cb), cb)
@@ -79,7 +88,7 @@
     def away(k, i):
         d = peer(i)
         return pltpu.make_async_remote_copy(
-            src_ref=stem.at[:, :, columns(d, k), :],
+            src_ref=staged.at[k, d],
             dst_ref=held.at[k, :, rows(me)],
             send_sem=out_send.at[k, i],
             recv_sem=out_recv.at[k, me],
@@ -89,12 +98,18 @@
 
     def arrival(k, s):
         return pltpu.make_async_remote_copy(
-            src_ref=stem.at[:, :, columns(0, k), :],
+            src_ref=staged.at[k, s],
             dst_ref=held.at[k, :, rows(s)],
             send_sem=out_send.at[k, 0],
             recv_sem=out_recv.at[k, s],
             device_id={"inter": s},
             device_id_type=MESH,
+        )
+
+    def stage(k, i):
+        d = peer(i)
+        return pltpu.make_async_copy(
+            stem.at[:, :, columns(d, k), :], staged.at[k, d], stage_sem.at[k, i]
         )
 
     def own_in(k):
@@ -131,6 +146,11 @@
     def weights_out():
         return pltpu.make_async_copy(shuffled, w_three, own_sem.at[2, 0])
 
+    for k in range(chunks):
+        @pl.loop(1, n)
+        def _(i):
+            stage(k, i).start()
+
     barrier = pltpu.get_barrier_semaphore()
 
     @pl.loop(1, n)
@@ -141,6 +161,7 @@
 
     @pl.loop(1, n)
     def _(i):
+        stage(0, i).wait()
         away(0, i).start()
 
     for k in range(chunks):
@@ -198,6 +219,7 @@
         @pl.loop(1, n)
         def _(i):
             away(k - 1, i).wait_send()
+            stage(k, i).wait()
             away(k, i).start()
 
     for k in range(chunks):
@@ -215,7 +237,7 @@
 
         @pl.loop(1, n)
         def _(i):
-            s = peer(n - i)
+            s = peer(i)
             arrival(k, s).wait_recv()
             turn(s)
 
@@ -268,7 +290,7 @@
         @pl.loop(1, n)
         def _(i):
             back(k, i).wait_send()
-            back_arrival(k, peer(n - i)).wait_recv()
+            back_arrival(k, peer(i)).wait_recv()
 
 
 def close_kernel(block_ref, w_three, out_ref):
@@ -316,6 +338,7 @@
         in_specs=[anywhere] + [vmem] * 8,
         out_specs=[anywhere, anywhere],
         scratch_shapes=[
+            pltpu.VMEM((CHUNKS, n, 2, la, cb, size_r), jnp.bfloat16),
             pltpu.VMEM((CHUNKS, 2, size_a, cb, size_r), jnp.bfloat16),
             pltpu.VMEM((cb, 2 * size_a, size_r), jnp.bfloat16),
             pltpu.VMEM((2 * size_a, 2 * size_a), jnp.bfloat16),
@@ -327,10 +350,11 @@
             pltpu.SemaphoreType.DMA((CHUNKS, n)),
             pltpu.SemaphoreType.DMA((CHUNKS, n)),
             pltpu.SemaphoreType.DMA((CHUNKS, n)),
+            pltpu.SemaphoreType.DMA((CHUNKS, n)),
             pltpu.SemaphoreType.DMA((3, CHUNKS)),
         ],
         compiler_params=pltpu.CompilerParams(
-            collective_id=0, has_side_effects=True, vmem_limit_bytes=56 * 1024 * 1024
+            collective_id=0, has_side_effects=True, vmem_limit_bytes=62 * 1024 * 1024
         ),
         cost_estimate=pl.CostEstimate(
             flops=24 * size_a * size_a * lb * size_r,
@@ -370,7 +394,7 @@
     lb = size_b // n
     fits = (
         amps == 1
-        and n > 1
+        and n % 2 == 0
         and la % 16 == 0
         and lb % (16 * CHUNKS) == 0
         and size_r == 256

time: 758 us -> 765 us (level)
  no operation moved by 1% of the time
where the time goes in v3:
time: 765 us
  Pallas kernels  765 us (100%)
    pallas_call x1, Pallas kernels, kernel_device(): pl.pallas_call(functools.partial(swap_kernel, n), out_shape=[jax.ShapeDty...  739 us
    pallas_call x1, Pallas kernels, kernel_device(): pl.pallas_call(close_kernel, grid=(la // steps,), out_shape=jax.ShapeDtyp...  25.8 us

profile of v3, /device:TPU:1, one launch (start us, length us, event | category | flops | bytes accessed | tf_op | source)
XLA Modules:
  0.0 764.7 jit_solution(14286339093076579269)
XLA Ops:
  0.0 738.9 %shard_map.91 = (bf16[2,16,2,32,16,256]{5,4,3,2,1,0:T(8,128)(2,1)}, bf16[1024,1024]{1,0:T(8,128)(2,1)}) custom-call(bf16[2,32,512,256]{3,2,1,0:T(8,128)(2,1)} %bitcast.3, bf16[2,512,512]{2,1,0:T(8,128)(2,1)} %branch_one.1, bf16[2,256,256]{2,1,0:T(8,128)(2,1)} %branch_two.1, s32[1,256]{1,0:T(1,128)} %bitcast.4, bf16[2,512,512]{2,1,0:T(8,128)(2,1)} %branch_three.1, ...), custom_call_target="tpu_custom_call" | custom-call | flops 51539607552 | bytes 67108864 | tf_op jit(solution)/shard_map/pallas_call | solution.py:332
  738.9 25.8 %shard_map.92 = f32[4096,2,8,128]{3,2,1,0:T(8,128)} custom-call(bf16[2,16,2,32,16,256]{5,4,3,2,1,0:T(8,128)(2,1)} %get-tuple-element.7.block_ref, bf16[1024,1024]{1,0:T(8,128)(2,1)} %get-tuple-element.8.w_three), custom_call_target="tpu_custom_call" | custom-call | flops 17179869184 | bytes 50331648 | tf_op jit(solution)/shard_map/pallas_call | solution.py:372

commit v4 on v3

--- a/solution.py
+++ b/solution.py
@@ -10,6 +10,7 @@
 
 MESH = pl.DeviceIdType.MESH
 CHUNKS = 2
+WINDOW = 4
 RUN = 64
 
 
@@ -65,6 +66,7 @@
     la = stem.shape[1]
     chunks, _, size_a, cb, size_r = held.shape
     lb = chunks * cb
+    window = min(WINDOW, n - 1)
     wing = n // 2
     base = me // wing * wing
     other = wing - base
@@ -162,6 +164,11 @@
     @pl.loop(1, n)
     def _(i):
         stage(0, i).wait()
+
+        @pl.when(i > window)
+        def _():
+            away(0, i - window).wait_send()
+
         away(0, i).start()
 
     for k in range(chunks):
@@ -215,15 +222,14 @@
         ).astype(jnp.bfloat16)
     weights_out().start()
 
-    for k in range(1, chunks):
-        @pl.loop(1, n)
-        def _(i):
-            away(k - 1, i).wait_send()
-            stage(k, i).wait()
-            away(k, i).start()
-
     for k in range(chunks):
         own_in(k).wait()
+        if k + 1 < chunks:
+            @pl.loop(1, window + 1)
+            def _(i):
+                away(k, n - 1 - window + i).wait_send()
+                stage(k + 1, i).wait()
+                away(k + 1, i).start()
 
         def turn(s):
             for p in range(2):
@@ -264,6 +270,12 @@
             )
             turned[b, :size_a] = both[:, :size_r]
             turned[b, size_a:] = both[:, size_r:]
+            if k + 1 < chunks:
+                @pl.when(b < n - 1 - window)
+                def _():
+                    away(k + 1, b + 1).wait_send()
+                    stage(k + 1, b + 1 + window).wait()
+                    away(k + 1, b + 1 + window).start()
 
         def unturn(d):
             for p in range(2):
@@ -277,7 +289,9 @@
         def _(i):
             unturn(peer(i))
             if k + 1 < chunks:
-                away(k + 1, i).wait_send()
+                @pl.when(i >= n - window)
+                def _():
+                    away(k + 1, i).wait_send()
             back(k, i).start()
 
         unturn(me)
@@ -395,6 +409,7 @@
     fits = (
         amps == 1
         and n % 2 == 0
+        and n - 1 - min(WINDOW, n - 1) <= lb // CHUNKS
         and la % 16 == 0
         and lb % (16 * CHUNKS) == 0
         and size_r == 256

time: 765 us -> 764 us (level)
  no operation moved by 1% of the time
where the time goes in v4:
time: 764 us; the launch traced here: 760 us
  Pallas kernels  760 us (99%)
    pallas_call x1, Pallas kernels, kernel_device(): pl.pallas_call(functools.partial(swap_kernel, n), out_shape=[jax.ShapeDty...  734 us
    pallas_call x1, Pallas kernels, kernel_device(): pl.pallas_call(close_kernel, grid=(la // steps,), out_shape=jax.ShapeDtyp...  25.8 us

profile of v4, /device:TPU:1, one launch (start us, length us, event | category | flops | bytes accessed | tf_op | source)
XLA Modules:
  0.0 759.6 jit_solution(16799975772327470270)
XLA Ops:
  0.0 733.8 %shard_map.91 = (bf16[2,16,2,32,16,256]{5,4,3,2,1,0:T(8,128)(2,1)}, bf16[1024,1024]{1,0:T(8,128)(2,1)}) custom-call(bf16[2,32,512,256]{3,2,1,0:T(8,128)(2,1)} %bitcast.3, bf16[2,512,512]{2,1,0:T(8,128)(2,1)} %branch_one.1, bf16[2,256,256]{2,1,0:T(8,128)(2,1)} %branch_two.1, s32[1,256]{1,0:T(1,128)} %bitcast.4, bf16[2,512,512]{2,1,0:T(8,128)(2,1)} %branch_three.1, ...), custom_call_target="tpu_custom_call" | custom-call | flops 51539607552 | bytes 67108864 | tf_op jit(solution)/shard_map/pallas_call | solution.py:346
  733.8 25.8 %shard_map.92 = f32[4096,2,8,128]{3,2,1,0:T(8,128)} custom-call(bf16[2,16,2,32,16,256]{5,4,3,2,1,0:T(8,128)(2,1)} %get-tuple-element.7.block_ref, bf16[1024,1024]{1,0:T(8,128)(2,1)} %get-tuple-element.8.w_three), custom_call_target="tpu_custom_call" | custom-call | flops 17179869184 | bytes 50331648 | tf_op jit(solution)/shard_map/pallas_call | solution.py:386
